TPU v7x, 32 devices: a whole 2x2x4 slice. The times are simulated.
32 devices in a mesh: dp: 16 (over z, y, x), tensor: 2 (over core).
Axes of the slice: x: 2, y: 2, z: 4, core: 2. Of those that a mesh axis runs over, the one named last changes fastest.
Arguments:
- image_in: bfloat16 [3200, 768], P(('dp', 'tensor')), may hold values from -6 to 6
- image_norm_gain: float32 [2, 2, 768], replicated, may hold values from 0.25 to 1.75
- image_norm_shift: float32 [2, 2, 768], replicated, may hold values from -3 to 3
- image_qkv: bfloat16 [2, 3, 768, 768], P(None, None, None, 'tensor'), may hold values from -0.21875 to 0.21875
- image_qv_bias: float32 [2, 2, 768], P(None, None, 'tensor'), may hold values from -3 to 3
- image_out_proj: bfloat16 [2, 768, 768], P(None, 'tensor'), may hold values from -0.875 to 0.875
- image_fc_in: bfloat16 [2, 768, 3072], P(None, None, 'tensor'), may hold values from -0.21875 to 0.21875
- image_fc_in_bias: float32 [2, 3072], P(None, 'tensor'), may hold values from -3 to 3
- image_fc_out: bfloat16 [2, 3072, 768], P(None, 'tensor'), may hold values from -0.109375 to 0.109375
- image_res_bias: float32 [2, 2, 768], replicated, may hold values from -3 to 3
- image_cot: float32 [3200, 768], P(('dp', 'tensor')), may hold values from -6 to 6
- caption_in: bfloat16 [2464, 512], P(('dp', 'tensor')), may hold values from -6 to 6
- caption_norm_gain: float32 [2, 2, 512], replicated, may hold values from 0.25 to 1.75
- caption_norm_shift: float32 [2, 2, 512], replicated, may hold values from -3 to 3
- caption_qkv: bfloat16 [2, 3, 512, 512], P(None, None, None, 'tensor'), may hold values from -0.25 to 0.25
- caption_qv_bias: float32 [2, 2, 512], P(None, None, 'tensor'), may hold values from -3 to 3
- caption_out_proj: bfloat16 [2, 512, 512], P(None, 'tensor'), may hold values from -1 to 1
- caption_fc_in: bfloat16 [2, 512, 2048], P(None, None, 'tensor'), may hold values from -0.25 to 0.25
- caption_fc_in_bias: float32 [2, 2048], P(None, 'tensor'), may hold values from -3 to 3
- caption_fc_out: bfloat16 [2, 2048, 512], P(None, 'tensor'), may hold values from -0.125 to 0.125
- caption_res_bias: float32 [2, 2, 512], replicated, may hold values from -3 to 3
- caption_lengths: int32 [32], P('dp'), may hold values from 5 to 77, as said below
- caption_cot: float32 [2464, 512], P(('dp', 'tensor')), may hold values from -6 to 6
Outputs:
- image_out: float32 [3200, 768], P(('dp', 'tensor'))
- image_in_grad: float32 [3200, 768], P(('dp', 'tensor'))
- image_norm_gain_grad: float32 [2, 2, 768], replicated
- image_norm_shift_grad: float32 [2, 2, 768], replicated
- image_qkv_grad: float32 [2, 3, 768, 768], P(None, None, 'dp', 'tensor')
- image_qv_bias_grad: float32 [2, 2, 768], replicated
- image_out_proj_grad: float32 [2, 768, 768], P(None, 'tensor', 'dp')
- image_fc_in_grad: float32 [2, 768, 3072], P(None, 'dp', 'tensor')
- image_fc_in_bias_grad: float32 [2, 3072], replicated
- image_fc_out_grad: float32 [2, 3072, 768], P(None, 'tensor', 'dp')
- image_res_bias_grad: float32 [2, 2, 768], replicated
- caption_out: float32 [2464, 512], P(('dp', 'tensor'))
- caption_in_grad: float32 [2464, 512], P(('dp', 'tensor'))
- caption_norm_gain_grad: float32 [2, 2, 512], replicated
- caption_norm_shift_grad: float32 [2, 2, 512], replicated
- caption_qkv_grad: float32 [2, 3, 512, 512], P(None, None, 'dp', 'tensor')
- caption_qv_bias_grad: float32 [2, 2, 512], replicated
- caption_out_proj_grad: float32 [2, 512, 512], P(None, 'tensor', 'dp')
- caption_fc_in_grad: float32 [2, 512, 2048], P(None, 'dp', 'tensor')
- caption_fc_in_bias_grad: float32 [2, 2048], replicated
- caption_fc_out_grad: float32 [2, 2048, 512], P(None, 'tensor', 'dp')
- caption_res_bias_grad: float32 [2, 2, 512], replicated
Inputs may be any that keep to these rules, and one draw needn't show every extreme that they name: `caption_lengths`: each caption's number of tokens; some caption has all 77.
All inputs are finite; a program needn't handle non-finite values.
Results may differ from a plain program's by a relative error of at most 0.02.
Values may be sent and summed in bfloat16 or wider, within the bound.
No kernel may reach another device: no remote copies, remote signals or barrier semaphores. Data moves between devices by JAX's collectives and lax.ppermute only.
A program may use at most 192 MiB of HBM per device.

v0:
```python
import jax
import jax.numpy as jnp
from jax import lax
from jax.sharding import PartitionSpec as P

DI = 768
FI = 3072
DT = 512
FT = 2048
HEAD = 64
PATCHES = 50
CTX = 77


EPS = 1e-05


def layer_norm(values, norm_gain, norm_shift):
    centred = values - jnp.mean(values, axis=-1, keepdims=True)
    spread = jnp.mean(centred * centred, axis=-1, keepdims=True)
    return centred * lax.rsqrt(spread + EPS) * norm_gain + norm_shift


def dot_plain(first, second):
    return jnp.dot(first, second, preferred_element_type=jnp.float32)


def dot_back(first, second):
    return lax.dot_general(
        first, second, (((1,), (1,)), ((), ())), preferred_element_type=jnp.float32
    )


def dot_over(first, second):
    return lax.dot_general(
        first, second, (((0,), (0,)), ((), ())), preferred_element_type=jnp.float32
    )


def gather_normed(values):
    return lax.all_gather(values, "tensor", axis=0, tiled=True)


def gather_grads(values):
    return lax.all_gather(values, "tensor", axis=0, tiled=True)


def sum_branch(operand, weight):
    row_share = operand.shape[0] // lax.axis_size("tensor")

    def term(first_row, row_count):
        return dot_plain(operand, weight)

    return lax.psum_scatter(
        term(jnp.int32(0), row_share * lax.axis_size("tensor")).astype(jnp.bfloat16),
        "tensor",
        scatter_dimension=0,
        tiled=True,
    ).astype(jnp.float32)


def sum_inputs(grad_list, weight_list):
    row_share = grad_list[0].shape[0] // lax.axis_size("tensor")

    def term(first_row, row_count):
        summed = jnp.zeros((row_count, weight_list[0].shape[0]), jnp.float32)
        for grad_part, weight in zip(grad_list, weight_list):
            summed = summed + dot_back(grad_part, weight)
        return summed

    return lax.psum_scatter(
        term(jnp.int32(0), row_share * lax.axis_size("tensor")).astype(jnp.bfloat16),
        "tensor",
        scatter_dimension=0,
        tiled=True,
    ).astype(jnp.float32)


def split_heads(values, seq_len):
    return values.reshape(values.shape[0] // seq_len, seq_len, values.shape[1] // HEAD, HEAD)


def softmax_probs(query_rows, key_rows, allowed, seq_len):
    scores = jnp.einsum(
        "gqhe,gkhe->ghqk",
        split_heads(query_rows, seq_len),
        split_heads(key_rows, seq_len),
        preferred_element_type=jnp.float32,
    ) * HEAD ** (-0.5)
    if allowed is not None:
        scores = jnp.where(allowed, scores, -1000000000.0)
    highest = jnp.max(scores, axis=-1, keepdims=True)
    weights = jnp.exp(scores - highest)
    return weights / jnp.sum(weights, axis=-1, keepdims=True)


def block_forward(inputs, index, params, allowed, seq_len):
    norm_gain, norm_shift, w_qkv, qv_bias, out_proj, fc_in, fc_in_bias, fc_out, res_bias = params
    normed = layer_norm(inputs, norm_gain[index, 0], norm_shift[index, 0]).astype(jnp.bfloat16)
    gathered = gather_normed(normed)
    query_rows = (dot_plain(gathered, w_qkv[index, 0]) + qv_bias[index, 0]).astype(jnp.bfloat16)
    key_rows = dot_plain(gathered, w_qkv[index, 1]).astype(jnp.bfloat16)
    value_rows = (dot_plain(gathered, w_qkv[index, 2]) + qv_bias[index, 1]).astype(jnp.bfloat16)
    probs = softmax_probs(query_rows, key_rows, allowed, seq_len)
    mixed_heads = jnp.einsum(
        "ghqk,gkhe->gqhe",
        probs.astype(jnp.bfloat16),
        split_heads(value_rows, seq_len),
        preferred_element_type=jnp.float32,
    )
    mixed = mixed_heads.reshape(query_rows.shape).astype(jnp.bfloat16)
    middle = inputs + sum_branch(mixed, out_proj[index]) + res_bias[index, 0]
    normed_two = layer_norm(middle, norm_gain[index, 1], norm_shift[index, 1]).astype(jnp.bfloat16)
    gathered_two = gather_normed(normed_two)
    hidden = dot_plain(gathered_two, fc_in[index]) + fc_in_bias[index]
    active = (hidden * jax.nn.sigmoid(1.702 * hidden)).astype(jnp.bfloat16)
    output = middle + sum_branch(active, fc_out[index]) + res_bias[index, 1]
    saved = (
        inputs,
        gathered,
        query_rows,
        key_rows,
        value_rows,
        probs,
        mixed,
        middle,
        gathered_two,
        hidden,
        active,
    )
    return (output, saved)


def block_backward(grad_out, index, params, saved, seq_len):
    norm_gain, norm_shift, w_qkv, qv_bias, out_proj, fc_in, fc_in_bias, fc_out, res_bias = params
    (
        inputs,
        gathered,
        query_rows,
        key_rows,
        value_rows,
        probs,
        mixed,
        middle,
        gathered_two,
        hidden,
        active,
    ) = saved
    grad_res_two = jnp.sum(grad_out, axis=0)
    grad_branch_two = gather_grads(grad_out.astype(jnp.bfloat16))
    grad_fc_out = dot_over(active, grad_branch_two)
    grad_active = dot_back(grad_branch_two, fc_out[index])
    sigma = jax.nn.sigmoid(1.702 * hidden)
    grad_hidden = (grad_active * (sigma + 1.702 * hidden * sigma * (1.0 - sigma))).astype(
        jnp.bfloat16
    )
    grad_fc_in_bias = jnp.sum(grad_hidden, axis=0, dtype=jnp.float32)
    grad_fc_in = dot_over(gathered_two, grad_hidden)
    grad_normed_two = sum_inputs((grad_hidden,), (fc_in[index],))
    pull_two = jax.vjp(layer_norm, middle, norm_gain[index, 1], norm_shift[index, 1])[1]
    grad_middle_part, grad_gain_two, grad_shift_two = pull_two(grad_normed_two)
    grad_middle = grad_out + grad_middle_part
    grad_res_one = jnp.sum(grad_middle, axis=0)
    grad_branch_one = gather_grads(grad_middle.astype(jnp.bfloat16))
    grad_out_proj = dot_over(mixed, grad_branch_one)
    grad_mixed = dot_back(grad_branch_one, out_proj[index]).astype(jnp.bfloat16)
    query_heads = split_heads(query_rows, seq_len)
    key_heads = split_heads(key_rows, seq_len)
    value_heads = split_heads(value_rows, seq_len)
    grad_heads = split_heads(grad_mixed, seq_len)
    grad_probs = jnp.einsum(
        "gqhe,gkhe->ghqk", grad_heads, value_heads, preferred_element_type=jnp.float32
    )
    grad_value = jnp.einsum(
        "ghqk,gqhe->gkhe",
        probs.astype(jnp.bfloat16),
        grad_heads,
        preferred_element_type=jnp.float32,
    )
    grad_value = grad_value.reshape(value_rows.shape).astype(jnp.bfloat16)
    grad_scores = (
        probs * (grad_probs - jnp.sum(probs * grad_probs, axis=-1, keepdims=True))
    ).astype(jnp.bfloat16)
    grad_query = jnp.einsum(
        "ghqk,gkhe->gqhe", grad_scores, key_heads, preferred_element_type=jnp.float32
    ) * HEAD ** (-0.5)
    grad_query = grad_query.reshape(query_rows.shape).astype(jnp.bfloat16)
    grad_key = jnp.einsum(
        "ghqk,gqhe->gkhe", grad_scores, query_heads, preferred_element_type=jnp.float32
    ) * HEAD ** (-0.5)
    grad_key = grad_key.reshape(key_rows.shape).astype(jnp.bfloat16)
    grad_qv_bias = jnp.stack(
        [
            jnp.sum(grad_query, axis=0, dtype=jnp.float32),
            jnp.sum(grad_value, axis=0, dtype=jnp.float32),
        ]
    )
    grad_qkv = jnp.stack(
        [
            dot_over(gathered, grad_query),
            dot_over(gathered, grad_key),
            dot_over(gathered, grad_value),
        ]
    )
    grad_normed = sum_inputs(
        (grad_query, grad_key, grad_value), (w_qkv[index, 0], w_qkv[index, 1], w_qkv[index, 2])
    )
    pull_one = jax.vjp(layer_norm, inputs, norm_gain[index, 0], norm_shift[index, 0])[1]
    grad_inputs_part, grad_gain_one, grad_shift_one = pull_one(grad_normed)
    grad_inputs = grad_middle + grad_inputs_part
    layer_grads = (
        jnp.stack([grad_gain_one, grad_gain_two]),
        jnp.stack([grad_shift_one, grad_shift_two]),
        grad_qkv,
        grad_qv_bias,
        grad_out_proj,
        grad_fc_in,
        grad_fc_in_bias,
        grad_fc_out,
        jnp.stack([grad_res_one, grad_res_two]),
    )
    return (grad_inputs, layer_grads)


def run_tower(inputs, params, cotangent, allowed, seq_len):
    depth_count = params[0].shape[0]
    stored = []
    kept = []
    state = inputs.astype(jnp.float32)
    for index in range(depth_count):
        stored.append(state)
        state, saved = block_forward(state, index, params, allowed, seq_len)
        kept.append(saved)
    grad_state = cotangent
    collected = []
    for index in reversed(range(depth_count)):
        saved = block_forward(stored[index], index, params, allowed, seq_len)[1]
        grad_state, layer_grads = block_backward(grad_state, index, params, saved, seq_len)
        collected.insert(0, layer_grads)
    stacked = tuple((jnp.stack([entry[member] for entry in collected]) for member in range(9)))
    return (state, grad_state, stacked)


def widen(values, full_width):
    placed = jnp.zeros(values.shape[:-1] + (full_width,), jnp.float32)
    return lax.dynamic_update_slice_in_dim(
        placed, values, lax.axis_index("tensor") * values.shape[-1], values.ndim - 1
    )


def on_device(
    image_in,
    image_norm_gain,
    image_norm_shift,
    image_qkv,
    image_qv_bias,
    image_out_proj,
    image_fc_in,
    image_fc_in_bias,
    image_fc_out,
    image_res_bias,
    image_cot,
    caption_in,
    caption_norm_gain,
    caption_norm_shift,
    caption_qkv,
    caption_qv_bias,
    caption_out_proj,
    caption_fc_in,
    caption_fc_in_bias,
    caption_fc_out,
    caption_res_bias,
    caption_lengths,
    caption_cot,
):
    image_params = (
        image_norm_gain,
        image_norm_shift,
        image_qkv,
        image_qv_bias,
        image_out_proj,
        image_fc_in,
        image_fc_in_bias,
        image_fc_out,
        image_res_bias,
    )
    caption_params = (
        caption_norm_gain,
        caption_norm_shift,
        caption_qkv,
        caption_qv_bias,
        caption_out_proj,
        caption_fc_in,
        caption_fc_in_bias,
        caption_fc_out,
        caption_res_bias,
    )
    spots = jnp.arange(CTX)
    caption_mask = (spots[None, None, None, :] <= spots[None, None, :, None]) & (
        spots[None, None, None, :] < caption_lengths[:, None, None, None]
    )
    image_out, image_grad, image_grads = run_tower(image_in, image_params, image_cot, None, PATCHES)
    caption_out, caption_grad, caption_grads = run_tower(
        caption_in, caption_params, caption_cot, caption_mask, CTX
    )
    summed = (
        lax.psum_scatter(image_grads[2], "dp", scatter_dimension=2, tiled=True),
        lax.psum_scatter(image_grads[4], "dp", scatter_dimension=2, tiled=True),
        lax.psum_scatter(image_grads[5], "dp", scatter_dimension=1, tiled=True),
        lax.psum_scatter(image_grads[7], "dp", scatter_dimension=2, tiled=True),
        lax.psum_scatter(caption_grads[2], "dp", scatter_dimension=2, tiled=True),
        lax.psum_scatter(caption_grads[4], "dp", scatter_dimension=2, tiled=True),
        lax.psum_scatter(caption_grads[5], "dp", scatter_dimension=1, tiled=True),
        lax.psum_scatter(caption_grads[7], "dp", scatter_dimension=2, tiled=True),
    )
    small = lax.psum(
        (
            image_grads[0],
            image_grads[1],
            widen(image_grads[3], DI),
            widen(image_grads[6], FI),
            image_grads[8],
            caption_grads[0],
            caption_grads[1],
            widen(caption_grads[3], DT),
            widen(caption_grads[6], FT),
            caption_grads[8],
        ),
        ("dp", "tensor"),
    )
    return (
        image_out,
        image_grad,
        small[0],
        small[1],
        summed[0],
        small[2],
        summed[1],
        summed[2],
        small[3],
        summed[3],
        small[4],
        caption_out,
        caption_grad,
        small[5],
        small[6],
        summed[4],
        small[7],
        summed[5],
        summed[6],
        small[8],
        summed[7],
        small[9],
    )


def solution(mesh):
    placed = (
        P(("dp", "tensor"), None),
        P(),
        P(),
        P(None, None, None, "tensor"),
        P(None, None, "tensor"),
        P(None, "tensor", None),
        P(None, None, "tensor"),
        P(None, "tensor"),
        P(None, "tensor", None),
        P(),
        P(("dp", "tensor"), None),
        P(("dp", "tensor"), None),
        P(),
        P(),
        P(None, None, None, "tensor"),
        P(None, None, "tensor"),
        P(None, "tensor", None),
        P(None, None, "tensor"),
        P(None, "tensor"),
        P(None, "tensor", None),
        P(),
        P("dp"),
        P(("dp", "tensor"), None),
    )
    return jax.shard_map(
        on_device,
        mesh=mesh,
        in_specs=placed,
        out_specs=(
            P(("dp", "tensor"), None),
            P(("dp", "tensor"), None),
            P(),
            P(),
            P(None, None, "dp", "tensor"),
            P(),
            P(None, "tensor", "dp"),
            P(None, "dp", "tensor"),
            P(),
            P(None, "tensor", "dp"),
            P(),
            P(("dp", "tensor"), None),
            P(("dp", "tensor"), None),
            P(),
            P(),
            P(None, None, "dp", "tensor"),
            P(),
            P(None, "tensor", "dp"),
            P(None, "dp", "tensor"),
            P(),
            P(None, "tensor", "dp"),
            P(),
        ),
        check_vma=False,
    )
```

profile of v0, /device:TPU:0, one launch (start us, length us, event | category | flops | bytes accessed | tf_op | source)
XLA Modules:
  0.0 1548.4 jit_solution(17562172743107629358)
XLA Ops:
  41.3 2.5 fusion.68
  48.5 3.9 fusion.352
  64.2 2.5 convolution_convert_fusion.11
  70.0 2.4 convolution_add_fusion.1
  73.6 3.2 fusion.59
  76.8 4.0 fusion.351
  113.7 2.4 fusion.376
  116.1 2.5 fusion.69
  122.1 4.5 fusion.350
  138.3 3.4 all-gather.12
  145.0 2.7 convert_reduce_fusion.6
  150.8 2.8 concatenate.2
  153.5 2.5 fusion.360
  160.7 4.4 all-gather.4
  166.8 2.5 convolution_add_fusion
  169.3 3.7 convert_reduce_fusion
  175.5 4.5 fusion.349
  180.7 2.8 collective-permute-start.12
  183.5 4.5 convolution_bitcast_fusion
  189.3 14.1 collective-permute-start.4
  203.4 2.8 concatenate.12
  220.9 2.8 convert_reduce_fusion.13
  253.2 3.0 convert_reduce_fusion.2
  269.5 3.9 fusion.348
  282.2 2.6 convert_reduce_fusion.7
  287.7 2.5 pad_maximum_fusion.4
  290.2 7.3 copy.220
  301.7 3.7 convert_reduce_fusion.1
  305.4 3.2 convolution_bitcast_fusion.1
  308.6 2.6 fusion.56
  311.2 3.3 fusion.347
  318.0 8.0 pad_maximum_fusion.1
  326.0 15.0 copy.186
  354.2 3.1 copy.185
  358.4 2.4 convolution_convert_fusion.10
  361.5 3.3 fusion.65
  389.8 2.5 convert_reduce_fusion.4
  403.7 5.1 fusion.346
  421.2 3.4 pad_maximum_fusion.5
  426.6 2.4 pad_maximum_fusion.3
  433.0 3.3 pad_maximum_fusion.2
  439.1 4.6 pad_maximum_fusion
  452.2 376.0 %all-reduce.50.cloned.1.call-done = (f32[2,384,768]{1,0,2:T(2,128)}, f32[2,1536,768]{1,0,2:T(2,128)}, f32[2,256,512]{1,0,2:T(2,128)}, f32[2,1024,512]{1,0,2:T(2,128)}) async-done(((f32[2,384,768]{1,0,2:T(2,128)}, f32[2,1536,768]{1,0,2:T(2,128)}, f32[2,256,512]{1,0,2:T(2,128)}, f32[2,1024,512]{1,0,2:T(2,128)}), (f32[2,384,768]{1,0,2:T(2,128)}, f32[2,1536,768]{1,0,2:T(2,128)}, f32[2,256,512]{1,0,2:T(2,128)}, ...) | async-done | bytes 17039376
  835.1 128.8 %all-reduce.48.cloned.1.call-done = (f32[2,2,768]{2,1,0:T(2,128)}, f32[2,2,768]{2,1,0:T(2,128)}, f32[2,2,768]{2,1,0:T(2,128)}, f32[2,3072]{1,0:T(2,128)}, f32[2,...) async-done(((f32[2,2,768]{2,1,0:T(2,128)}, f32[2,2,768]{2,1,0:T(2,128)}, ...) | async-done | bytes 122896 | tf_op jit(solution)/shard_map/psum | solution.py:316
  963.9 135.6 %reduce-scatter.41.cloned.1.call-done = f32[2,3,32,256]{3,2,1,0:T(8,128)} async-done(((f32[2,3,512,256]{3,2,1,0:T(8,128)}), f32[2,3,32,256]{3,2,1,0:T(8,128)}) %reduce-scatter.41.cloned.1.call-update) | async-done | bytes 196624 | tf_op jit(solution)/shard_map/reduce_scatter | solution.py:311
  1099.6 97.1 %reduce-scatter.43.cloned.1.call-done = f32[2,32,1024]{2,1,0:T(8,128)} async-done(((f32[2,512,1024]{2,1,0:T(8,128)}), f32[2,32,1024]{2,1,0:T(8,128)}) %reduce-scatter.43.cloned.1.call-update) | async-done | bytes 262160 | tf_op jit(solution)/shard_map/reduce_scatter | solution.py:313
  1196.7 155.7 %reduce-scatter.37.cloned.1.call-done = f32[2,3,48,384]{3,2,1,0:T(8,128)} async-done(((f32[2,3,768,384]{3,2,1,0:T(8,128)}), f32[2,3,48,384]{3,2,1,0:T(8,128)}) %reduce-scatter.37.cloned.1.call-update) | async-done | bytes 442384 | tf_op jit(solution)/shard_map/reduce_scatter | solution.py:307
  1352.4 175.9 %reduce-scatter.39.cloned.1.call-done = f32[2,48,1536]{2,1,0:T(8,128)} async-done(((f32[2,768,1536]{2,1,0:T(8,128)}), f32[2,48,1536]{2,1,0:T(8,128)}) %reduce-scatter.39.cloned.1.call-update) | async-done | bytes 589840 | tf_op jit(solution)/shard_map/reduce_scatter | solution.py:309
  (847 shorter events, 292.5 us)
Async XLA Ops:
  7.2 18.1 %copy-start.8 = (bf16[2,3,512,256]{3,2,1,0:T(8,128)(2,1)S(1)}, bf16[2,3,512,256]{3,2,1,0:T(8,128)(2,1)}, u32[]{:S(2)}) copy-start(bf16[2,3,512,256]{3,2,1,0:T(8,128)(2,1)} %param.37) | copy-start | bytes 4718596
  7.2 821.0 %all-reduce.50.cloned.1.call-start = ((), (), s32[]{:S(2)}) async-start(), calls=%async_computation.9 | async-start | bytes 34078720
  9.2 17.6 %copy-start.128 = (f32[100]{0:T(128)}, f32[100]{0:T(128)S(1)}, u32[]{:S(2)}) copy-start(f32[100]{0:T(128)S(1)} %broadcast_multiply_fusion.7) | copy-start | bytes 1204
  10.3 16.5 %copy-start.164 = (f32[100]{0:T(128)}, f32[100]{0:T(128)S(1)}, u32[]{:S(2)}) copy-start(f32[100]{0:T(128)S(1)} %fusion.274) | copy-start | bytes 1204
  10.3 16.5 %copy-start = (bf16[100,768]{1,0:T(8,128)(2,1)S(1)}, bf16[100,768]{1,0:T(8,128)(2,1)}, u32[]{:S(2)}) copy-start(bf16[100,768]{1,0:T(8,128)(2,1)} %param.23) | copy-start | bytes 460804
  16.0 68.9 %copy-start.98 = (f32[1,1,512]{2,1,0:T(1,128)}, f32[1,1,512]{2,1,0:T(1,128)S(1)}, u32[]{:S(2)}) copy-start(f32[1,1,512]{2,1,0:T(1,128)S(1)} %get-tuple-element.209) | copy-start | bytes 6148
  43.8 14.0 copy-start.205
  43.8 16.2 %copy-start.1 = (bf16[77,512]{1,0:T(8,128)(2,1)S(1)}, bf16[77,512]{1,0:T(8,128)(2,1)}, u32[]{:S(2)}) copy-start(bf16[77,512]{1,0:T(8,128)(2,1)} %param.34) | copy-start | bytes 236548
  45.2 18.9 %copy-start.38 = (bf16[200,384]{1,0:T(8,128)(2,1)}, bf16[200,384]{1,0:T(8,128)(2,1)S(1)}, u32[]{:S(2)}) copy-start(bf16[200,384]{1,0:T(8,128)(2,1)S(1)} %convert_element_type.526) | copy-start | bytes 460804
  52.4 7.3 collective-permute-start.8
  54.7 12.0 collective-permute-start
  80.8 3.4 collective-permute-start.9
  82.9 16.1 %collective-permute-start.1 = (bf16[4,768]{1,0:T(4,128)(2,1)S(1)}, bf16[4,768]{1,0:T(4,128)(2,1)S(1)}, u32[]{:S(2)}, u32[]{:S(2)}) collective-permute-start(bf16[4,768]{1,0:T(4,128)(2,1)S(1)} %slice.325), channel_id=1, source_target_pairs={{0,1},{2,3},{4,5},{6,7},{8,9},{10,11},{12,13},{14,15},{16,17},{18,... | collective-permute-start | bytes 18440
  118.5 16.7 %copy-start.157 = (f32[1,1,512]{2,1,0:T(1,128)S(1)}, f32[1,1,512]{2,1,0:T(1,128)}, u32[]{:S(2)}) copy-start(f32[1,1,512]{2,1,0:T(1,128)} %get-tuple-element.210) | copy-start | bytes 6148
  127.3 4.0 collective-permute-start.10
  129.4 21.4 %collective-permute-start.2 = (bf16[4,768]{1,0:T(4,128)(2,1)S(1)}, bf16[4,768]{1,0:T(4,128)(2,1)}, u32[]{:S(2)}, u32[]{:S(2)}) collective-permute-start(bf16[4,768]{1,0:T(4,128)(2,1)S(1)} %slice.326), channel_id=1, source_target_pairs={{0,1},{2,3},{4,5},{6,7},{8,9},{10,11},{12,13},{14,15},{16,17},{18,... | collective-permute-start | bytes 18440
  180.7 27.2 %copy-start.171 = (f32[77]{0:T(128)S(1)}, f32[77]{0:T(128)}, u32[]{:S(2)}) copy-start(f32[77]{0:T(128)} %copy-done.170) | copy-start | bytes 928
  180.7 22.7 %collective-permute-start.12 = (bf16[3,512]{1,0:T(4,128)(2,1)S(1)}, bf16[3,512]{1,0:T(4,128)(2,1)}, u32[]{:S(2)}, u32[]{:S(2)}) collective-permute-start(bf16[3,512]{1,0:T(4,128)(2,1)S(1)} %slice.336), channel_id=1, source_target_pairs={{0,1},{2,3},{4,5},{6,7},{8,9},{10,11},{12,13},{14,15},{16,17},{18,... | collective-permute-start | bytes 9224
  189.3 54.5 %collective-permute-start.4 = (bf16[4,768]{1,0:T(4,128)(2,1)}, bf16[4,768]{1,0:T(4,128)(2,1)}, u32[]{:S(2)}, u32[]{:S(2)}) collective-permute-start(bf16[4,768]{1,0:T(4,128)(2,1)} %slice.328), channel_id=1, source_target_pairs={{0,1},{2,3},{4,5},{6,7},{8,9},{10,11},{12,13},{14,15},{16,17},{18,... | collective-permute-start | bytes 18440
  273.4 4.8 collective-permute-start.13
  277.0 20.6 %collective-permute-start.5 = (bf16[4,768]{1,0:T(4,128)(2,1)S(1)}, bf16[4,768]{1,0:T(4,128)(2,1)S(1)}, u32[]{:S(2)}, u32[]{:S(2)}) collective-permute-start(bf16[4,768]{1,0:T(4,128)(2,1)S(1)} %slice.329), channel_id=1, source_target_pairs={{0,1},{2,3},{4,5},{6,7},{8,9},{10,11},{12,13},{14,15},{16,17},{18,... | collective-permute-start | bytes 18440
  314.6 26.4 %collective-permute-start.14 = (bf16[3,512]{1,0:T(4,128)(2,1)S(1)}, bf16[3,512]{1,0:T(4,128)(2,1)S(1)}, u32[]{:S(2)}, u32[]{:S(2)}) collective-permute-start(bf16[3,512]{1,0:T(4,128)(2,1)S(1)} %slice.338), channel_id=1, source_target_pairs={{0,1},{2,3},{4,5},{6,7},{8,9},{10,11},{12,13},{14,15},{16,17},{18,... | collective-permute-start | bytes 9224
  316.7 30.6 %collective-permute-start.6 = (bf16[4,768]{1,0:T(4,128)(2,1)S(1)}, bf16[4,768]{1,0:T(4,128)(2,1)S(1)}, u32[]{:S(2)}, u32[]{:S(2)}) collective-permute-start(bf16[4,768]{1,0:T(4,128)(2,1)S(1)} %slice.330), channel_id=1, source_target_pairs={{0,1},{2,3},{4,5},{6,7},{8,9},{10,11},{12,13},{14,15},{16,17},{18,... | collective-permute-start | bytes 18440
  326.0 15.3 copy-start.131
  326.0 15.5 %copy-start.197 = (f32[77]{0:T(128)S(1)}, f32[77]{0:T(128)}, u32[]{:S(2)}) copy-start(f32[77]{0:T(128)} %copy-done.196) | copy-start | bytes 928
  326.0 15.5 %copy-start.167 = (f32[77]{0:T(128)S(1)}, f32[77]{0:T(128)}, u32[]{:S(2)}) copy-start(f32[77]{0:T(128)} %copy-done.166) | copy-start | bytes 928
  326.0 16.3 %copy-start.31 = (f32[77,512]{1,0:T(8,128)S(1)}, f32[77,512]{1,0:T(8,128)}, u32[]{:S(2)}) copy-start(f32[77,512]{1,0:T(8,128)} %copy-done.30) | copy-start | bytes 473092
  357.3 606.6 %all-reduce.48.cloned.1.call-start = ((), (), s32[]{:S(2)}) async-start(), calls=%async_computation.8 | async-start | bytes 245760 | tf_op jit(solution)/shard_map/psum | solution.py:316
  400.5 13.8 copy-start.120
  400.5 13.8 copy-start.119
  402.0 14.1 copy-start.173
  402.0 14.3 copy-start.151
  402.0 14.3 copy-start.150
  402.0 14.4 copy-start.125
  402.0 15.0 copy-start.126
  402.1 16.6 %copy-start.93 = (f32[768]{0:T(1024)S(1)}, f32[768]{0:T(1024)}, u32[]{:S(2)}) copy-start(f32[768]{0:T(1024)} %copy-done.92) | copy-start | bytes 9220
  402.1 16.6 %copy-start.129 = (f32[100]{0:T(128)S(1)}, f32[100]{0:T(128)}, u32[]{:S(2)}) copy-start(f32[100]{0:T(128)} %copy-done.128) | copy-start | bytes 1204
  402.1 17.5 %copy-start.165 = (f32[100]{0:T(128)S(1)}, f32[100]{0:T(128)}, u32[]{:S(2)}) copy-start(f32[100]{0:T(128)} %copy-done.164) | copy-start | bytes 1204
  402.1 17.8 %copy-start.102 = (f32[1,2,768]{2,1,0:T(2,128)S(1)}, f32[1,2,768]{2,1,0:T(2,128)}, u32[]{:S(2)}) copy-start(f32[1,2,768]{2,1,0:T(2,128)} %maximum_bitcast_fusion.5) | copy-start | bytes 18436
  402.1 18.4 %copy-start.103 = (f32[1,2,768]{2,1,0:T(2,128)S(1)}, f32[1,2,768]{2,1,0:T(2,128)}, u32[]{:S(2)}) copy-start(f32[1,2,768]{2,1,0:T(2,128)} %maximum_bitcast_fusion.7) | copy-start | bytes 18436
  410.2 4.1 collective-permute-start.15
  412.3 5.4 collective-permute-start.7
  421.1 678.4 %reduce-scatter.41.cloned.1.call-start = ((), (), s32[]{:S(2)}) async-start(), calls=%async_computation.6 | async-start | bytes 3342336 | tf_op jit(solution)/shard_map/reduce_scatter | solution.py:311
  424.6 772.1 %reduce-scatter.43.cloned.1.call-start = ((), (), s32[]{:S(2)}) async-start(), calls=%async_computation.7 | async-start | bytes 4456448 | tf_op jit(solution)/shard_map/reduce_scatter | solution.py:313
  429.1 923.4 %reduce-scatter.37.cloned.1.call-start = ((), (), s32[]{:S(2)}) async-start(), calls=%async_computation.4 | async-start | bytes 7520256 | tf_op jit(solution)/shard_map/reduce_scatter | solution.py:307
  436.3 1092.0 %reduce-scatter.39.cloned.1.call-start = ((), (), s32[]{:S(2)}) async-start(), calls=%async_computation.5 | async-start | bytes 10027008 | tf_op jit(solution)/shard_map/reduce_scatter | solution.py:309
  443.8 4.7 collective-permute-start.11
  447.1 3.1 collective-permute-start.3
  (188 other events, 938.6 us)
Sparse Core Ops, SparseCore 0:
  357.5 470.7 all-reduce.49
  837.5 126.3 all-reduce.47
  969.5 130.0 reduce-scatter.40
  1102.3 94.3 reduce-scatter.42
  1202.4 149.9 reduce-scatter.36
  1358.5 169.7 reduce-scatter.38
where the time goes:
time: 1560 us; the launch traced here: 1550 us
  waiting for transfers between devices  1070 us (69%)
  local copies, waits for them, and re-layouts  142 us (9%)
  matrix products  138 us (9%)
  other arithmetic  72.6 us (5%)
  blocking collectives  65.8 us (4%)
  starting transfers between devices  41.2 us (3%)
  between operations  20.2 us (1%)
    unnamed x23, waiting for transfers between devices  376 us
    reduce_scatter x1, waiting for transfers between devices, on_device(): lax.psum_scatter(image_grads[5], 'dp', scatter_dimension=1, tiled=True)  176 us
    reduce_scatter x1, waiting for transfers between devices, on_device(): lax.psum_scatter(image_grads[2], 'dp', scatter_dimension=2, tiled=True)  156 us
    reduce_scatter x1, waiting for transfers between devices, on_device(): lax.psum_scatter(caption_grads[2], 'dp', scatter_dimension=2, tiled=True)  136 us
    psum x1, waiting for transfers between devices, on_device(): lax.psum((image_grads[0], image_grads[1], widen(image_grads[3], DI), wide...  129 us
    reduce_scatter x1, waiting for transfers between devices, on_device(): lax.psum_scatter(caption_grads[5], 'dp', scatter_dimension=1, tiled=True)  97.1 us
    unnamed x496, local copies, waits for them, and re-layouts  59.6 us
    unnamed x17, starting transfers between devices  40.4 us
  transfers between devices with their start and end apart: 22, of which 6 were waited for; matrix products, arithmetic and copies ran while one was open for 13% of the time, Pallas kernels for 0%

commit v1 on v0

--- a/solution.py
+++ b/solution.py
@@ -131,7 +131,7 @@
     return (output, saved)
 
 
-def block_backward(grad_out, index, params, saved, seq_len):
+def block_backward(grad_out, index, params, saved, seq_len, orders):
     norm_gain, norm_shift, w_qkv, qv_bias, out_proj, fc_in, fc_in_bias, fc_out, res_bias = params
     (
         inputs,
@@ -148,21 +148,22 @@
     ) = saved
     grad_res_two = jnp.sum(grad_out, axis=0)
     grad_branch_two = gather_grads(grad_out.astype(jnp.bfloat16))
-    grad_fc_out = dot_over(active, grad_branch_two)
     grad_active = dot_back(grad_branch_two, fc_out[index])
     sigma = jax.nn.sigmoid(1.702 * hidden)
     grad_hidden = (grad_active * (sigma + 1.702 * hidden * sigma * (1.0 - sigma))).astype(
         jnp.bfloat16
     )
     grad_fc_in_bias = jnp.sum(grad_hidden, axis=0, dtype=jnp.float32)
-    grad_fc_in = dot_over(gathered_two, grad_hidden)
     grad_normed_two = sum_inputs((grad_hidden,), (fc_in[index],))
     pull_two = jax.vjp(layer_norm, middle, norm_gain[index, 1], norm_shift[index, 1])[1]
     grad_middle_part, grad_gain_two, grad_shift_two = pull_two(grad_normed_two)
     grad_middle = grad_out + grad_middle_part
     grad_res_one = jnp.sum(grad_middle, axis=0)
     grad_branch_one = gather_grads(grad_middle.astype(jnp.bfloat16))
-    grad_out_proj = dot_over(mixed, grad_branch_one)
+    grad_fc_out, grad_out_proj = sum_matrices(
+        [(grad_branch_two, active), (grad_branch_one, mixed)], orders[0]
+    )
+    grad_fc_out, grad_out_proj = grad_fc_out.T, grad_out_proj.T
     grad_mixed = dot_back(grad_branch_one, out_proj[index]).astype(jnp.bfloat16)
     query_heads = split_heads(query_rows, seq_len)
     key_heads = split_heads(key_rows, seq_len)
@@ -195,13 +196,16 @@
             jnp.sum(grad_value, axis=0, dtype=jnp.float32),
         ]
     )
-    grad_qkv = jnp.stack(
+    grad_fc_in, grad_query_w, grad_key_w, grad_value_w = sum_matrices(
         [
-            dot_over(gathered, grad_query),
-            dot_over(gathered, grad_key),
-            dot_over(gathered, grad_value),
-        ]
-    )
+            (gathered_two, grad_hidden),
+            (gathered, grad_query),
+            (gathered, grad_key),
+            (gathered, grad_value),
+        ],
+        orders[1],
+    )
+    grad_qkv = jnp.stack([grad_query_w, grad_key_w, grad_value_w])
     grad_normed = sum_inputs(
         (grad_query, grad_key, grad_value), (w_qkv[index, 0], w_qkv[index, 1], w_qkv[index, 2])
     )
@@ -222,20 +226,75 @@
     return (grad_inputs, layer_grads)
 
 
-def run_tower(inputs, params, cotangent, allowed, seq_len):
+def dp_bits():
+    return (lax.axis_size("dp") - 1).bit_length()
+
+
+def slice_order(order):
+    me = lax.axis_index("dp")
+    places = jnp.arange(lax.axis_size("dp"))
+    source = jnp.zeros_like(places)
+    for digit, bit in enumerate(order):
+        source = source | (((places >> (len(order) - 1 - digit)) & 1) << bit)
+    return source ^ me
+
+
+def pick_matrix(width, order):
+    depth = width // lax.axis_size("dp")
+    wanted = jnp.repeat(slice_order(order) * depth, depth) + jnp.tile(
+        jnp.arange(depth), lax.axis_size("dp")
+    )
+    return (jnp.arange(width)[:, None] == wanted[None, :]).astype(jnp.bfloat16)
+
+
+def swap(values, bit):
+    size = lax.axis_size("dp")
+    return lax.ppermute(values, "dp", [(spot, spot ^ (1 << bit)) for spot in range(size)])
+
+
+def sum_matrices(pairs, order):
+    picks = pick_matrix(pairs[0][0].shape[1], order)
+    terms = [
+        dot_over(dot_plain(left, picks).astype(jnp.bfloat16), right) for left, right in pairs
+    ]
+    total = jnp.concatenate(terms, axis=1)
+    for bit in order:
+        half = total.shape[0] // 2
+        total = total[:half] + swap(total[half:].astype(jnp.bfloat16), bit).astype(jnp.float32)
+    cuts = []
+    first = 0
+    for _, right in pairs:
+        cuts.append(total[:, first : first + right.shape[1]])
+        first += right.shape[1]
+    return cuts
+
+
+def sum_small(members):
+    flat = jnp.concatenate([member.reshape(-1) for member in members])
+    flat = flat + lax.ppermute(flat, "tensor", [(0, 1), (1, 0)])
+    for bit in range(dp_bits()):
+        flat = flat + swap(flat, bit)
+    parts = []
+    first = 0
+    for member in members:
+        parts.append(flat[first : first + member.size].reshape(member.shape))
+        first += member.size
+    return parts
+
+
+def run_tower(inputs, params, cotangent, allowed, seq_len, orders):
     depth_count = params[0].shape[0]
-    stored = []
     kept = []
     state = inputs.astype(jnp.float32)
     for index in range(depth_count):
-        stored.append(state)
         state, saved = block_forward(state, index, params, allowed, seq_len)
         kept.append(saved)
     grad_state = cotangent
     collected = []
     for index in reversed(range(depth_count)):
-        saved = block_forward(stored[index], index, params, allowed, seq_len)[1]
-        grad_state, layer_grads = block_backward(grad_state, index, params, saved, seq_len)
+        grad_state, layer_grads = block_backward(
+            grad_state, index, params, kept[index], seq_len, orders[index]
+        )
         collected.insert(0, layer_grads)
     stacked = tuple((jnp.stack([entry[member] for entry in collected]) for member in range(9)))
     return (state, grad_state, stacked)
@@ -299,21 +358,18 @@
     caption_mask = (spots[None, None, None, :] <= spots[None, None, :, None]) & (
         spots[None, None, None, :] < caption_lengths[:, None, None, None]
     )
-    image_out, image_grad, image_grads = run_tower(image_in, image_params, image_cot, None, PATCHES)
+    bits = list(range(dp_bits()))
+    first_way, second_way = bits, [1, 0] + bits[2:]
+    orders = [(first_way, second_way), (second_way, first_way)]
     caption_out, caption_grad, caption_grads = run_tower(
-        caption_in, caption_params, caption_cot, caption_mask, CTX
-    )
-    summed = (
-        lax.psum_scatter(image_grads[2], "dp", scatter_dimension=2, tiled=True),
-        lax.psum_scatter(image_grads[4], "dp", scatter_dimension=2, tiled=True),
-        lax.psum_scatter(image_grads[5], "dp", scatter_dimension=1, tiled=True),
-        lax.psum_scatter(image_grads[7], "dp", scatter_dimension=2, tiled=True),
-        lax.psum_scatter(caption_grads[2], "dp", scatter_dimension=2, tiled=True),
-        lax.psum_scatter(caption_grads[4], "dp", scatter_dimension=2, tiled=True),
-        lax.psum_scatter(caption_grads[5], "dp", scatter_dimension=1, tiled=True),
-        lax.psum_scatter(caption_grads[7], "dp", scatter_dimension=2, tiled=True),
-    )
-    small = lax.psum(
+        caption_in, caption_params, caption_cot, caption_mask, CTX, orders
+    )
+    image_out, image_grad, image_grads = run_tower(
+        image_in, image_params, image_cot, None, PATCHES, orders
+    )
+    summed = [image_grads[member] for member in (2, 4, 5, 7)]
+    summed += [caption_grads[member] for member in (2, 4, 5, 7)]
+    small = sum_small(
         (
             image_grads[0],
             image_grads[1],
@@ -325,8 +381,7 @@
             widen(caption_grads[3], DT),
             widen(caption_grads[6], FT),
             caption_grads[8],
-        ),
-        ("dp", "tensor"),
+        )
     )
     return (
         image_out,

time: 1560 us -> 712 us (0.46)
  waiting for transfers between devices: 1070 us -> 184 us
  matrix products: 138 us -> 181 us
  starting transfers between devices: 41.2 us -> 74.6 us
  local copies, waits for them, and re-layouts: 142 us -> 116 us
    reduce_scatter x4 -> x0, waiting for transfers between devices: 564 us -> none  [the longest x1 176 us: on_device(): lax.psum_scatter(image_grads[5], 'dp', scatter_dimension=1, tiled=True)]
    unnamed x23 -> x16, waiting for transfers between devices: 376 us -> 0.04 us
    ppermute x0 -> x37, waiting for transfers between devices: none -> 184 us  [the longest x36 184 us: swap(): lax.ppermute(values, 'dp', [(spot, spot ^ 1 << bit) for spot in range(siz...]
    psum x1 -> x0, waiting for transfers between devices: 129 us -> none  [on_device(): lax.psum((image_grads[0], image_grads[1], widen(image_grads[3], DI), wide...]
    ppermute x0 -> x37, starting transfers between devices: none -> 45.6 us  [the longest x36 45.6 us: swap(): lax.ppermute(values, 'dp', [(spot, spot ^ 1 << bit) for spot in range(siz...]
    dot_general x24, matrix products: 19.8 us -> 57.3 us  [dot_over(): lax.dot_general(first, second, (((0,), (0,)), ((), ())), preferred_elemen...]
    another operation x6 -> x14, local copies, waits for them, and re-layouts: 26.7 us -> 1.45 us  [run_tower(): jnp.stack([entry[member] for entry in collected])]
    another operation x34 -> x31, other arithmetic: 36.6 us -> 11.7 us  [run_tower(): jnp.stack([entry[member] for entry in collected])]
  transfers between devices with their start and end apart: 22 -> 53, of which waited for: 6 -> 25; matrix products, arithmetic and copies ran while one was open for 13% -> 42% of each run, Pallas kernels for 0% -> 0%
where the time goes in v1:
time: 712 us; the launch traced here: 699 us
  waiting for transfers between devices  184 us (26%)
  matrix products  181 us (25%)
  local copies, waits for them, and re-layouts  116 us (16%)
  starting transfers between devices  74.6 us (10%)
  other arithmetic  73.5 us (10%)
  blocking collectives  63.3 us (9%)
    ppermute x36, waiting for transfers between devices, swap(): lax.ppermute(values, 'dp', [(spot, spot ^ 1 << bit) for spot in range(siz...  184 us
    dot_general x24, matrix products, dot_over(): lax.dot_general(first, second, (((0,), (0,)), ((), ())), preferred_elemen...  57.3 us
    dot_general x24, matrix products, dot_back(): lax.dot_general(first, second, (((1,), (1,)), ((), ())), preferred_elemen...  49 us
    unnamed x508, local copies, waits for them, and re-layouts  46.7 us
    ppermute x36, starting transfers between devices, swap(): lax.ppermute(values, 'dp', [(spot, spot ^ 1 << bit) for spot in range(siz...  45.6 us
    dot_general x28, matrix products, dot_plain(): return jnp.dot(first, second, preferred_element_type=jnp.float32)  38.6 us
    unnamed x16, starting transfers between devices  29 us
    unnamed x7, blocking collectives  27.5 us
  transfers between devices with their start and end apart: 53, of which 25 were waited for; matrix products, arithmetic and copies ran while one was open for 42% of the time, Pallas kernels for 0%

profile of v1, /device:TPU:0, one launch (start us, length us, event | category | flops | bytes accessed | tf_op | source)
XLA Modules:
  0.0 699.0 jit_solution(11198365094083043040)
XLA Ops:
  32.4 3.3 fusion.426
  61.3 3.2 fusion.87
  64.6 4.0 fusion.425
  97.6 3.9 fusion.424
  118.9 3.2 convert_reduce_fusion.6
  122.1 3.3 fusion.142
  141.0 4.4 all-gather.4
  149.7 3.7 fusion.93
  155.8 4.9 fusion.112
  160.8 3.5 fusion.90
  164.2 4.5 fusion.423
  170.1 2.9 collective-permute-start.48
  172.9 4.7 fusion.110
  267.2 3.3 fusion.422
  273.9 3.0 fusion.24
  278.2 4.1 pad_maximum_fusion.1
  294.8 3.5 fusion.140
  311.6 4.5 convert_reduce_fusion.1
  316.1 4.8 fusion.109
  321.0 3.5 fusion.84
  324.5 4.8 fusion.113
  329.3 3.9 fusion.421
  418.6 4.5 fusion.420
  425.2 4.1 pad_maximum_fusion
  429.3 3.2 copy-done.2
  435.6 3.0 fusion.25
  454.2 3.4 collective-permute-done.2
  462.5 3.1 collective-permute-start.4
  466.4 3.4 collective-permute-done.4
  479.0 30.2 %collective-permute-done.29 = bf16[256,1280]{1,0:T(8,128)(2,1)} collective-permute-done((bf16[256,1280]{1,0:T(8,128)(2,1)}, bf16[256,1280]{1,0:T(8,128)(2,1)}, u32[]{:S(2)}, u32[]{:S(2)}) %collective-permute-start.29) | collective-permute-done | bytes 655392 | tf_op jit(solution)/shard_map/ppermute | solution.py:252
  515.8 33.9 %collective-permute-done.34 = bf16[128,1280]{1,0:T(8,128)(2,1)S(1)} collective-permute-done((bf16[128,1280]{1,0:T(8,128)(2,1)S(1)}, bf16[128,1280]{1,0:T(8,128)(2,1)S(1)}, u32[]{:S(2)}, u32[]{:S(2)}) %collective-permute-start.34) | collective-permute-done | bytes 327712 | tf_op jit(solution)/shard_map/ppermute | solution.py:252
  551.3 12.7 %collective-permute-done.30 = bf16[128,1280]{1,0:T(8,128)(2,1)S(1)} collective-permute-done((bf16[128,1280]{1,0:T(8,128)(2,1)S(1)}, bf16[128,1280]{1,0:T(8,128)(2,1)S(1)}, u32[]{:S(2)}, u32[]{:S(2)}) %collective-permute-start.30) | collective-permute-done | bytes 327712 | tf_op jit(solution)/shard_map/ppermute | solution.py:252
  565.9 3.6 collective-permute-done.35
  571.3 4.3 collective-permute-done.31
  575.7 2.8 collective-permute-start.36
  578.5 4.2 collective-permute-done.36
  583.9 5.1 collective-permute-done.32
  592.1 5.3 collective-permute-done.26
  599.3 9.6 %collective-permute-done.22 = bf16[128,1792]{1,0:T(8,128)(2,1)S(1)} collective-permute-done((bf16[128,1792]{1,0:T(8,128)(2,1)S(1)}, bf16[128,1792]{1,0:T(8,128)(2,1)S(1)}, u32[]{:S(2)}, u32[]{:S(2)}) %collective-permute-start.22) | collective-permute-done | bytes 458784 | tf_op jit(solution)/shard_map/ppermute | solution.py:252
  618.8 6.3 collective-permute-done.28
  625.1 6.4 collective-permute-done.24
  642.1 5.4 collective-permute-done.19
  648.0 8.9 %collective-permute-done.15 = bf16[96,1920]{1,0:T(8,128)(2,1)S(1)} collective-permute-done((bf16[96,1920]{1,0:T(8,128)(2,1)S(1)}, bf16[96,1920]{1,0:T(8,128)(2,1)S(1)}, u32[]{:S(2)}, u32[]{:S(2)}) %collective-permute-start.15) | collective-permute-done | bytes 368672 | tf_op jit(solution)/shard_map/ppermute | solution.py:252
  657.2 12.2 %collective-permute-done.16 = bf16[48,1920]{1,0:T(8,128)(2,1)S(1)} collective-permute-done((bf16[48,1920]{1,0:T(8,128)(2,1)S(1)}, bf16[48,1920]{1,0:T(8,128)(2,1)S(1)}, u32[]{:S(2)}, u32[]{:S(2)}) %collective-permute-start.16) | collective-permute-done | bytes 184352 | tf_op jit(solution)/shard_map/ppermute | solution.py:252
  673.7 8.2 %collective-permute-done.11 = bf16[96,2688]{1,0:T(8,128)(2,1)S(1)} collective-permute-done((bf16[96,2688]{1,0:T(8,128)(2,1)S(1)}, bf16[96,2688]{1,0:T(8,128)(2,1)S(1)}, u32[]{:S(2)}, u32[]{:S(2)}) %collective-permute-start.11) | collective-permute-done | bytes 516128 | tf_op jit(solution)/shard_map/ppermute | solution.py:252
  682.1 5.4 collective-permute-done.7
  687.7 3.5 collective-permute-done.12
  691.4 5.4 collective-permute-done.8
  (1037 shorter events, 409.6 us)
Async XLA Ops:
  35.7 12.8 %collective-permute-start.45 = (bf16[3,512]{1,0:T(4,128)(2,1)S(1)}, bf16[3,512]{1,0:T(4,128)(2,1)S(1)}, u32[]{:S(2)}, u32[]{:S(2)}) collective-permute-start(bf16[3,512]{1,0:T(4,128)(2,1)S(1)} %slice.912), channel_id=1, source_target_pairs={{0,1},{2,3},{4,5},{6,7},{8,9},{10,11},{12,13},{14,15},{16,17},{18,... | collective-permute-start | bytes 9224
  38.0 16.9 %collective-permute-start.37 = (bf16[4,768]{1,0:T(4,128)(2,1)S(1)}, bf16[4,768]{1,0:T(4,128)(2,1)S(1)}, u32[]{:S(2)}, u32[]{:S(2)}) collective-permute-start(bf16[4,768]{1,0:T(4,128)(2,1)S(1)} %slice.904), channel_id=1, source_target_pairs={{0,1},{2,3},{4,5},{6,7},{8,9},{10,11},{12,13},{14,15},{16,17},{18,... | collective-permute-start | bytes 18440
  70.9 11.5 %collective-permute-start.38 = (bf16[4,768]{1,0:T(4,128)(2,1)S(1)}, bf16[4,768]{1,0:T(4,128)(2,1)S(1)}, u32[]{:S(2)}, u32[]{:S(2)}) collective-permute-start(bf16[4,768]{1,0:T(4,128)(2,1)S(1)} %slice.905), channel_id=1, source_target_pairs={{0,1},{2,3},{4,5},{6,7},{8,9},{10,11},{12,13},{14,15},{16,17},{18,... | collective-permute-start | bytes 18440
  102.3 5.7 collective-permute-start.47
  104.4 27.5 %collective-permute-start.39 = (bf16[4,768]{1,0:T(4,128)(2,1)S(1)}, bf16[4,768]{1,0:T(4,128)(2,1)S(1)}, u32[]{:S(2)}, u32[]{:S(2)}) collective-permute-start(bf16[4,768]{1,0:T(4,128)(2,1)S(1)} %slice.906), channel_id=1, source_target_pairs={{0,1},{2,3},{4,5},{6,7},{8,9},{10,11},{12,13},{14,15},{16,17},{18,... | collective-permute-start | bytes 18440
  170.1 12.6 %collective-permute-start.48 = (bf16[3,512]{1,0:T(4,128)(2,1)}, bf16[3,512]{1,0:T(4,128)(2,1)}, u32[]{:S(2)}, u32[]{:S(2)}) collective-permute-start(bf16[3,512]{1,0:T(4,128)(2,1)} %slice.915), channel_id=1, source_target_pairs={{0,1},{2,3},{4,5},{6,7},{8,9},{10,11},{12,13},{14,15},{16,17},{18,... | collective-permute-start | bytes 9224
  178.9 58.3 %collective-permute-start.41 = (bf16[4,768]{1,0:T(4,128)(2,1)}, bf16[4,768]{1,0:T(4,128)(2,1)}, u32[]{:S(2)}, u32[]{:S(2)}) collective-permute-start(bf16[4,768]{1,0:T(4,128)(2,1)} %slice.908), channel_id=1, source_target_pairs={{0,1},{2,3},{4,5},{6,7},{8,9},{10,11},{12,13},{14,15},{16,17},{18,... | collective-permute-start | bytes 18440
  228.4 247.5 %collective-permute-start.33 = (bf16[256,1280]{1,0:T(8,128)(2,1)}, bf16[256,1280]{1,0:T(8,128)(2,1)}, u32[]{:S(2)}, u32[]{:S(2)}) collective-permute-start(bf16[256,1280]{1,0:T(8,128)(2,1)} %fusion.62), channel_id=1, source_target_pairs={{0,4},{2,6},{4,0},{6,2},{8,12},{10,14},{12,8},{14,10},{16,20},{18,... | collective-permute-start | bytes 1966088 | tf_op jit(solution)/shard_map/ppermute | solution.py:252
  234.3 276.5 %collective-permute-start.25 = (bf16[256,1792]{1,0:T(8,128)(2,1)}, bf16[256,1792]{1,0:T(8,128)(2,1)}, u32[]{:S(2)}, u32[]{:S(2)}) collective-permute-start(bf16[256,1792]{1,0:T(8,128)(2,1)} %slice.1254), channel_id=1, source_target_pairs={{0,2},{2,0},{4,6},{6,4},{8,10},{10,8},{12,14},{14,12},{16,18},{18,... | collective-permute-start | bytes 2752520 | tf_op jit(solution)/shard_map/ppermute | solution.py:252
  270.5 17.6 %collective-permute-start.49 = (bf16[3,512]{1,0:T(4,128)(2,1)S(1)}, bf16[3,512]{1,0:T(4,128)(2,1)S(1)}, u32[]{:S(2)}, u32[]{:S(2)}) collective-permute-start(bf16[3,512]{1,0:T(4,128)(2,1)S(1)} %slice.916), channel_id=1, source_target_pairs={{0,1},{2,3},{4,5},{6,7},{8,9},{10,11},{12,13},{14,15},{16,17},{18,... | collective-permute-start | bytes 9224
  272.6 31.4 %collective-permute-start.42 = (bf16[4,768]{1,0:T(4,128)(2,1)S(1)}, bf16[4,768]{1,0:T(4,128)(2,1)S(1)}, u32[]{:S(2)}, u32[]{:S(2)}) collective-permute-start(bf16[4,768]{1,0:T(4,128)(2,1)S(1)} %slice.909), channel_id=1, source_target_pairs={{0,1},{2,3},{4,5},{6,7},{8,9},{10,11},{12,13},{14,15},{16,17},{18,... | collective-permute-start | bytes 18440
  276.9 332.2 %collective-permute-start.17 = (bf16[384,1920]{1,0:T(8,128)(2,1)}, bf16[384,1920]{1,0:T(8,128)(2,1)}, u32[]{:S(2)}, u32[]{:S(2)}) collective-permute-start(bf16[384,1920]{1,0:T(8,128)(2,1)} %fusion.24), channel_id=1, source_target_pairs={{0,4},{2,6},{4,0},{6,2},{8,12},{10,14},{12,8},{14,10},{16,20},{18,... | collective-permute-start | bytes 4423688 | tf_op jit(solution)/shard_map/ppermute | solution.py:252
  333.3 8.3 %collective-permute-start.50 = (bf16[3,512]{1,0:T(4,128)(2,1)S(1)}, bf16[3,512]{1,0:T(4,128)(2,1)}, u32[]{:S(2)}, u32[]{:S(2)}) collective-permute-start(bf16[3,512]{1,0:T(4,128)(2,1)S(1)} %slice.917), channel_id=1, source_target_pairs={{0,1},{2,3},{4,5},{6,7},{8,9},{10,11},{12,13},{14,15},{16,17},{18,... | collective-permute-start | bytes 9224
  336.5 50.7 %collective-permute-start.43 = (bf16[4,768]{1,0:T(4,128)(2,1)}, bf16[4,768]{1,0:T(4,128)(2,1)}, u32[]{:S(2)}, u32[]{:S(2)}) collective-permute-start(bf16[4,768]{1,0:T(4,128)(2,1)} %slice.910), channel_id=1, source_target_pairs={{0,1},{2,3},{4,5},{6,7},{8,9},{10,11},{12,13},{14,15},{16,17},{18,... | collective-permute-start | bytes 18440
  423.1 15.7 %collective-permute-start.51 = (bf16[3,512]{1,0:T(4,128)(2,1)S(1)}, bf16[3,512]{1,0:T(4,128)(2,1)S(1)}, u32[]{:S(2)}, u32[]{:S(2)}) collective-permute-start(bf16[3,512]{1,0:T(4,128)(2,1)S(1)} %slice.918), channel_id=1, source_target_pairs={{0,1},{2,3},{4,5},{6,7},{8,9},{10,11},{12,13},{14,15},{16,17},{18,... | collective-permute-start | bytes 9224
  434.0 7.0 collective-permute-start.52
  441.0 5.2 collective-permute-start.40
  445.4 6.3 collective-permute-start.1
  446.2 186.8 %collective-permute-start.9 = (bf16[384,2688]{1,0:T(8,128)(2,1)}, bf16[384,2688]{1,0:T(8,128)(2,1)}, u32[]{:S(2)}, u32[]{:S(2)}) collective-permute-start(bf16[384,2688]{1,0:T(8,128)(2,1)} %slice.1250), channel_id=1, source_target_pairs={{0,2},{2,0},{4,6},{6,4},{8,10},{10,8},{12,14},{14,12},{16,18},{18,... | collective-permute-start | bytes 6193160 | tf_op jit(solution)/shard_map/ppermute | solution.py:252
  462.5 7.2 %collective-permute-start.4 = (f32[30720]{0:T(1024)S(1)}, f32[30720]{0:T(1024)S(1)}, u32[]{:S(2)}, u32[]{:S(2)}) collective-permute-start(f32[30720]{0:T(1024)S(1)} %add.793), channel_id=1, source_target_pairs={{0,16},{2,18},{4,20},{6,22},{8,24},{10,26},{12,28},{14,30},{16,0},... | collective-permute-start | bytes 368648 | tf_op jit(solution)/shard_map/ppermute | solution.py:252
  469.8 39.4 %collective-permute-start.29 = (bf16[256,1280]{1,0:T(8,128)(2,1)}, bf16[256,1280]{1,0:T(8,128)(2,1)}, u32[]{:S(2)}, u32[]{:S(2)}) collective-permute-start(bf16[256,1280]{1,0:T(8,128)(2,1)} %fusion.63), channel_id=1, source_target_pairs={{0,2},{2,0},{4,6},{6,4},{8,10},{10,8},{12,14},{14,12},{16,18},{18,... | collective-permute-start | bytes 1966088 | tf_op jit(solution)/shard_map/ppermute | solution.py:252
  476.0 38.1 %collective-permute-start.21 = (bf16[256,1792]{1,0:T(8,128)(2,1)}, bf16[256,1792]{1,0:T(8,128)(2,1)S(1)}, u32[]{:S(2)}, u32[]{:S(2)}) collective-permute-start(bf16[256,1792]{1,0:T(8,128)(2,1)} %slice.1255), channel_id=1, source_target_pairs={{0,4},{2,6},{4,0},{6,2},{8,12},{10,14},{12,8},{14,10},{16,20},{18,... | collective-permute-start | bytes 2752520 | tf_op jit(solution)/shard_map/ppermute | solution.py:252
  509.2 104.0 %collective-permute-start.13 = (bf16[384,1920]{1,0:T(8,128)(2,1)S(1)}, bf16[384,1920]{1,0:T(8,128)(2,1)S(1)}, u32[]{:S(2)}, u32[]{:S(2)}) collective-permute-start(bf16[384,1920]{1,0:T(8,128)(2,1)S(1)} %copy-done.32), channel_id=1, source_target_pairs={{0,2},{2,0},{4,6},{6,4},{8,10},{10,8},{12,14},{14,12},{16,18},{18,... | collective-permute-start | bytes 4423688 | tf_op jit(solution)/shard_map/ppermute | solution.py:252
  510.8 126.7 %collective-permute-start.5 = (bf16[384,2688]{1,0:T(8,128)(2,1)S(1)}, bf16[384,2688]{1,0:T(8,128)(2,1)S(1)}, u32[]{:S(2)}, u32[]{:S(2)}) collective-permute-start(bf16[384,2688]{1,0:T(8,128)(2,1)S(1)} %copy-done.29), channel_id=1, source_target_pairs={{0,4},{2,6},{4,0},{6,2},{8,12},{10,14},{12,8},{14,10},{16,20},{18,... | collective-permute-start | bytes 6193160 | tf_op jit(solution)/shard_map/ppermute | solution.py:252
  514.1 35.7 %collective-permute-start.34 = (bf16[128,1280]{1,0:T(8,128)(2,1)S(1)}, bf16[128,1280]{1,0:T(8,128)(2,1)S(1)}, u32[]{:S(2)}, u32[]{:S(2)}) collective-permute-start(bf16[128,1280]{1,0:T(8,128)(2,1)S(1)} %slice.1264), channel_id=1, source_target_pairs={{0,2},{2,0},{4,6},{6,4},{8,10},{10,8},{12,14},{14,12},{16,18},{18,... | collective-permute-start | bytes 983048 | tf_op jit(solution)/shard_map/ppermute | solution.py:252
  549.7 14.3 %collective-permute-start.30 = (bf16[128,1280]{1,0:T(8,128)(2,1)S(1)}, bf16[128,1280]{1,0:T(8,128)(2,1)S(1)}, u32[]{:S(2)}, u32[]{:S(2)}) collective-permute-start(bf16[128,1280]{1,0:T(8,128)(2,1)S(1)} %slice.1265), channel_id=1, source_target_pairs={{0,4},{2,6},{4,0},{6,2},{8,12},{10,14},{12,8},{14,10},{16,20},{18,... | collective-permute-start | bytes 983048 | tf_op jit(solution)/shard_map/ppermute | solution.py:252
  564.0 5.5 collective-permute-start.35
  569.5 6.2 collective-permute-start.31
  575.7 7.1 %collective-permute-start.36 = (bf16[32,1280]{1,0:T(8,128)(2,1)S(1)}, bf16[32,1280]{1,0:T(8,128)(2,1)S(1)}, u32[]{:S(2)}, u32[]{:S(2)}) collective-permute-start(bf16[32,1280]{1,0:T(8,128)(2,1)S(1)} %slice.1276), channel_id=1, source_target_pairs={{0,16},{2,18},{4,20},{6,22},{8,24},{10,26},{12,28},{14,30},{16,0},... | collective-permute-start | bytes 245768 | tf_op jit(solution)/shard_map/ppermute | solution.py:252
  582.7 6.2 collective-permute-start.32
  589.0 8.5 %collective-permute-start.26 = (bf16[128,1792]{1,0:T(8,128)(2,1)S(1)}, bf16[128,1792]{1,0:T(8,128)(2,1)S(1)}, u32[]{:S(2)}, u32[]{:S(2)}) collective-permute-start(bf16[128,1792]{1,0:T(8,128)(2,1)S(1)} %slice.1260), channel_id=1, source_target_pairs={{0,4},{2,6},{4,0},{6,2},{8,12},{10,14},{12,8},{14,10},{16,20},{18,... | collective-permute-start | bytes 1376264 | tf_op jit(solution)/shard_map/ppermute | solution.py:252
  597.4 11.5 %collective-permute-start.22 = (bf16[128,1792]{1,0:T(8,128)(2,1)S(1)}, bf16[128,1792]{1,0:T(8,128)(2,1)S(1)}, u32[]{:S(2)}, u32[]{:S(2)}) collective-permute-start(bf16[128,1792]{1,0:T(8,128)(2,1)S(1)} %slice.1261), channel_id=1, source_target_pairs={{0,2},{2,0},{4,6},{6,4},{8,10},{10,8},{12,14},{14,12},{16,18},{18,... | collective-permute-start | bytes 1376264 | tf_op jit(solution)/shard_map/ppermute | solution.py:252
  609.0 7.2 %collective-permute-start.27 = (bf16[64,1792]{1,0:T(8,128)(2,1)S(1)}, bf16[64,1792]{1,0:T(8,128)(2,1)S(1)}, u32[]{:S(2)}, u32[]{:S(2)}) collective-permute-start(bf16[64,1792]{1,0:T(8,128)(2,1)S(1)} %slice.1268), channel_id=1, source_target_pairs={{0,8},{2,10},{4,12},{6,14},{8,0},{10,2},{12,4},{14,6},{16,24},{18,... | collective-permute-start | bytes 688136 | tf_op jit(solution)/shard_map/ppermute | solution.py:252
  609.1 9.6 %collective-permute-start.23 = (bf16[64,1792]{1,0:T(8,128)(2,1)S(1)}, bf16[64,1792]{1,0:T(8,128)(2,1)S(1)}, u32[]{:S(2)}, u32[]{:S(2)}) collective-permute-start(bf16[64,1792]{1,0:T(8,128)(2,1)S(1)} %slice.1269), channel_id=1, source_target_pairs={{0,8},{2,10},{4,12},{6,14},{8,0},{10,2},{12,4},{14,6},{16,24},{18,... | collective-permute-start | bytes 688136 | tf_op jit(solution)/shard_map/ppermute | solution.py:252
  613.2 26.4 %collective-permute-start.18 = (bf16[192,1920]{1,0:T(8,128)(2,1)S(1)}, bf16[192,1920]{1,0:T(8,128)(2,1)S(1)}, u32[]{:S(2)}, u32[]{:S(2)}) collective-permute-start(bf16[192,1920]{1,0:T(8,128)(2,1)S(1)} %slice.1256), channel_id=1, source_target_pairs={{0,2},{2,0},{4,6},{6,4},{8,10},{10,8},{12,14},{14,12},{16,18},{18,... | collective-permute-start | bytes 2211848 | tf_op jit(solution)/shard_map/ppermute | solution.py:252
  616.2 23.6 %collective-permute-start.14 = (bf16[192,1920]{1,0:T(8,128)(2,1)S(1)}, bf16[192,1920]{1,0:T(8,128)(2,1)S(1)}, u32[]{:S(2)}, u32[]{:S(2)}) collective-permute-start(bf16[192,1920]{1,0:T(8,128)(2,1)S(1)} %slice.1257), channel_id=1, source_target_pairs={{0,4},{2,6},{4,0},{6,2},{8,12},{10,14},{12,8},{14,10},{16,20},{18,... | collective-permute-start | bytes 2211848 | tf_op jit(solution)/shard_map/ppermute | solution.py:252
  618.7 6.4 collective-permute-start.28
  625.0 6.5 collective-permute-start.24
  635.3 35.7 %collective-permute-start.10 = (bf16[192,2688]{1,0:T(8,128)(2,1)S(1)}, bf16[192,2688]{1,0:T(8,128)(2,1)S(1)}, u32[]{:S(2)}, u32[]{:S(2)}) collective-permute-start(bf16[192,2688]{1,0:T(8,128)(2,1)S(1)} %slice.1252), channel_id=1, source_target_pairs={{0,4},{2,6},{4,0},{6,2},{8,12},{10,14},{12,8},{14,10},{16,20},{18,... | collective-permute-start | bytes 3096584 | tf_op jit(solution)/shard_map/ppermute | solution.py:252
  638.0 33.4 %collective-permute-start.6 = (bf16[192,2688]{1,0:T(8,128)(2,1)S(1)}, bf16[192,2688]{1,0:T(8,128)(2,1)S(1)}, u32[]{:S(2)}, u32[]{:S(2)}) collective-permute-start(bf16[192,2688]{1,0:T(8,128)(2,1)S(1)} %slice.1253), channel_id=1, source_target_pairs={{0,2},{2,0},{4,6},{6,4},{8,10},{10,8},{12,14},{14,12},{16,18},{18,... | collective-permute-start | bytes 3096584 | tf_op jit(solution)/shard_map/ppermute | solution.py:252
  639.8 7.8 %collective-permute-start.19 = (bf16[96,1920]{1,0:T(8,128)(2,1)S(1)}, bf16[96,1920]{1,0:T(8,128)(2,1)S(1)}, u32[]{:S(2)}, u32[]{:S(2)}) collective-permute-start(bf16[96,1920]{1,0:T(8,128)(2,1)S(1)} %slice.1262), channel_id=1, source_target_pairs={{0,8},{2,10},{4,12},{6,14},{8,0},{10,2},{12,4},{14,6},{16,24},{18,... | collective-permute-start | bytes 1105928 | tf_op jit(solution)/shard_map/ppermute | solution.py:252
  640.0 16.9 %collective-permute-start.15 = (bf16[96,1920]{1,0:T(8,128)(2,1)S(1)}, bf16[96,1920]{1,0:T(8,128)(2,1)S(1)}, u32[]{:S(2)}, u32[]{:S(2)}) collective-permute-start(bf16[96,1920]{1,0:T(8,128)(2,1)S(1)} %slice.1263), channel_id=1, source_target_pairs={{0,8},{2,10},{4,12},{6,14},{8,0},{10,2},{12,4},{14,6},{16,24},{18,... | collective-permute-start | bytes 1105928 | tf_op jit(solution)/shard_map/ppermute | solution.py:252
  647.6 9.5 %collective-permute-start.20 = (bf16[48,1920]{1,0:T(8,128)(2,1)S(1)}, bf16[48,1920]{1,0:T(8,128)(2,1)S(1)}, u32[]{:S(2)}, u32[]{:S(2)}) collective-permute-start(bf16[48,1920]{1,0:T(8,128)(2,1)S(1)} %slice.1270), channel_id=1, source_target_pairs={{0,16},{2,18},{4,20},{6,22},{8,24},{10,26},{12,28},{14,30},{16,0},... | collective-permute-start | bytes 552968 | tf_op jit(solution)/shard_map/ppermute | solution.py:252
  657.0 12.3 %collective-permute-start.16 = (bf16[48,1920]{1,0:T(8,128)(2,1)S(1)}, bf16[48,1920]{1,0:T(8,128)(2,1)S(1)}, u32[]{:S(2)}, u32[]{:S(2)}) collective-permute-start(bf16[48,1920]{1,0:T(8,128)(2,1)S(1)} %slice.1271), channel_id=1, source_target_pairs={{0,16},{2,18},{4,20},{6,22},{8,24},{10,26},{12,28},{14,30},{16,0},... | collective-permute-start | bytes 552968 | tf_op jit(solution)/shard_map/ppermute | solution.py:252
  671.2 10.6 %collective-permute-start.11 = (bf16[96,2688]{1,0:T(8,128)(2,1)S(1)}, bf16[96,2688]{1,0:T(8,128)(2,1)S(1)}, u32[]{:S(2)}, u32[]{:S(2)}) collective-permute-start(bf16[96,2688]{1,0:T(8,128)(2,1)S(1)} %slice.1258), channel_id=1, source_target_pairs={{0,8},{2,10},{4,12},{6,14},{8,0},{10,2},{12,4},{14,6},{16,24},{18,... | collective-permute-start | bytes 1548296 | tf_op jit(solution)/shard_map/ppermute | solution.py:252
  671.6 15.9 %collective-permute-start.7 = (bf16[96,2688]{1,0:T(8,128)(2,1)S(1)}, bf16[96,2688]{1,0:T(8,128)(2,1)S(1)}, u32[]{:S(2)}, u32[]{:S(2)}) collective-permute-start(bf16[96,2688]{1,0:T(8,128)(2,1)S(1)} %slice.1259), channel_id=1, source_target_pairs={{0,8},{2,10},{4,12},{6,14},{8,0},{10,2},{12,4},{14,6},{16,24},{18,... | collective-permute-start | bytes 1548296 | tf_op jit(solution)/shard_map/ppermute | solution.py:252
  682.0 9.3 %collective-permute-start.12 = (bf16[48,2688]{1,0:T(8,128)(2,1)S(1)}, bf16[48,2688]{1,0:T(8,128)(2,1)S(1)}, u32[]{:S(2)}, u32[]{:S(2)}) collective-permute-start(bf16[48,2688]{1,0:T(8,128)(2,1)S(1)} %slice.1266), channel_id=1, source_target_pairs={{0,16},{2,18},{4,20},{6,22},{8,24},{10,26},{12,28},{14,30},{16,0},... | collective-permute-start | bytes 774152 | tf_op jit(solution)/shard_map/ppermute | solution.py:252
  687.6 9.2 %collective-permute-start.8 = (bf16[48,2688]{1,0:T(8,128)(2,1)S(1)}, bf16[48,2688]{1,0:T(8,128)(2,1)S(1)}, u32[]{:S(2)}, u32[]{:S(2)}) collective-permute-start(bf16[48,2688]{1,0:T(8,128)(2,1)S(1)} %slice.1267), channel_id=1, source_target_pairs={{0,16},{2,18},{4,20},{6,22},{8,24},{10,26},{12,28},{14,30},{16,0},... | collective-permute-start | bytes 774152 | tf_op jit(solution)/shard_map/ppermute | solution.py:252
  (227 other events, 2341.5 us)
